TPU v7x, 32 devices: a whole 2x2x4 slice. The times are simulated.
32 devices in a mesh: seq: 16 (over z, y, core), head: 2 (over x).
Axes of the slice: x: 2, y: 2, z: 4, core: 2. Of those that a mesh axis runs over, the one named last changes fastest.
Arguments:
- query_tensor: float32 [8192, 32, 128], P('seq', 'head'), may hold values from -6 to 6
- key_tensor: float32 [8192, 16, 128], P('seq', 'head'), may hold values from -6 to 6
- value_tensor: float32 [8192, 16, 128], P('seq', 'head'), may hold values from -6 to 6
- output_gradient: float32 [8192, 32, 128], P('seq', 'head'), may hold values from -24 to 24
- logsumexp: float32 [32, 8192], P('head', 'seq'), may hold values from 5.5 to 7
- row_inner_products: float32 [32, 8192], P('head', 'seq'), may hold values from -120 to 120
Outputs:
- query_grad: float32 [8192, 32, 128], P('seq', 'head')
- key_grad: float32 [8192, 16, 128], P('seq', 'head')
- value_grad: float32 [8192, 16, 128], P('seq', 'head')
All inputs are finite; a program needn't handle non-finite values.
Results may differ from a plain program's by a relative error of at most 0.0053.
Values may be sent and summed in bfloat16 or wider, within the bound.
A program may use at most 192 MiB of HBM per device.

v0:
```python
import jax
import jax.numpy as jnp
from jax import lax
from jax.sharding import PartitionSpec as P

WINDOW = 1024
QSCALE = 168


def shifted(x, axis, by):
    count = lax.axis_size(axis)
    pairs = [(i, i + by) for i in range(count) if 0 <= i + by < count]
    return lax.ppermute(x, axis, pairs)


def probe(query_rows, gradient_list, lse_rows, output_dots, keys, values, offset, usable):
    window_length = query_rows.shape[0]
    span = keys.shape[0]
    scale = QSCALE ** (-0.5)
    scores = jnp.einsum("tkgd,skd->kgts", query_rows, keys, preferred_element_type=jnp.float32)
    qpos = lax.broadcasted_iota(jnp.int32, (window_length, span), 0) + offset
    kpos = lax.broadcasted_iota(jnp.int32, (window_length, span), 1)
    spread = qpos - kpos
    allowed = (spread >= 0) & (spread < WINDOW) & usable
    probs = jnp.where(allowed, jnp.exp(scale * scores - lse_rows[..., None]), 0.0)
    dprob = jnp.einsum("tkgd,skd->kgts", gradient_list, values, preferred_element_type=jnp.float32)
    dscore = probs * (dprob - output_dots[..., None])
    return (probs.astype(jnp.bfloat16), dscore.astype(jnp.bfloat16))


def query_term(dscore, keys):
    scale = QSCALE ** (-0.5)
    return scale * jnp.einsum("kgts,skd->tkgd", dscore, keys, preferred_element_type=jnp.float32)


def owner_terms(probs, dscore, query_rows, gradient_list):
    scale = QSCALE ** (-0.5)
    dvalue = jnp.einsum("kgts,tkgd->skd", probs, gradient_list, preferred_element_type=jnp.float32)
    dkey = scale * jnp.einsum(
        "kgts,tkgd->skd", dscore, query_rows, preferred_element_type=jnp.float32
    )
    return (dkey, dvalue)


def on_device(
    query_tensor, key_tensor, value_tensor, output_gradient, logsumexp, row_inner_products
):
    window_length, qheads, width = query_tensor.shape
    kheads = key_tensor.shape[1]
    query_group = qheads // kheads
    position = lax.axis_index("seq")
    local = (
        query_tensor.astype(jnp.bfloat16).reshape(window_length, kheads, query_group, width),
        output_gradient.astype(jnp.bfloat16).reshape(window_length, kheads, query_group, width),
        logsumexp.reshape(kheads, query_group, window_length),
        row_inner_products.reshape(kheads, query_group, window_length),
    )
    keys_low = key_tensor.astype(jnp.bfloat16)
    values_low = value_tensor.astype(jnp.bfloat16)
    near_keys, near_values = shifted((keys_low, values_low), "seq", 1)
    far_keys, far_values = shifted((keys_low, values_low), "seq", 2)
    probs, dscore = probe(*local, keys_low, values_low, 0, position >= 0)
    query_grad = query_term(dscore, keys_low)
    key_grad, value_grad = owner_terms(probs, dscore, local[0], local[1])
    probs, dscore = probe(*local, near_keys, near_values, window_length, position >= 1)
    query_grad = query_grad + query_term(dscore, near_keys)
    near_dkey, near_dvalue = owner_terms(probs, dscore, local[0], local[1])
    probs, dscore = probe(*local, far_keys, far_values, 2 * window_length, position >= 2)
    query_grad = query_grad + query_term(dscore, far_keys)
    far_dkey, far_dvalue = owner_terms(probs, dscore, local[0], local[1])
    back_dkey, back_dvalue = shifted((near_dkey, near_dvalue), "seq", -1)
    later_dkey, later_dvalue = shifted((far_dkey, far_dvalue), "seq", -2)
    key_grad = key_grad + back_dkey + later_dkey
    value_grad = value_grad + back_dvalue + later_dvalue
    return (query_grad.reshape(window_length, qheads, width), key_grad, value_grad)


def solution(mesh):
    return jax.shard_map(
        on_device,
        mesh=mesh,
        in_specs=(
            P("seq", "head", None),
            P("seq", "head", None),
            P("seq", "head", None),
            P("seq", "head", None),
            P("head", "seq"),
            P("head", "seq"),
        ),
        out_specs=(P("seq", "head", None), P("seq", "head", None), P("seq", "head", None)),
        check_vma=False,
    )
```

profile of v0, /device:TPU:0, one launch (start us, length us, event | category | flops | bytes accessed | tf_op | source)
XLA Modules:
  0.0 263.1 jit_solution(11498354380172231486)
XLA Ops:
  0.7 3.1 %copy.70 = bf16[512,8,128]{2,0,1:T(8,128)(2,1)} copy(f32[512,8,128]{2,1,0:T(8,128)} %param.8) | data formatting | bytes 3145728 | tf_op args[2]
  3.8 5.9 %collective-permute-start.3 = (bf16[512,8,128]{2,0,1:T(8,128)(2,1)}, bf16[512,8,128]{2,0,1:T(8,128)(2,1)}, u32[]{:S(2)}, u32[]{:S(2)}) collective-permute-start(bf16[512,8,128]{2,0,1:T(8,128)(2,1)} %copy.70), channel_id=1, source_target_pairs={{0,4},{2,6},{4,8},{6,10},{8,12},{10,14},{12,16},{14,18},{16,20},{1... | collective-permute-start | bytes 3145736 | tf_op jit(solution)/shard_map/ppermute | solution.py:13
  13.4 3.1 %collective-permute-start = (bf16[512,8,128]{2,0,1:T(8,128)(2,1)}, bf16[512,8,128]{2,0,1:T(8,128)(2,1)}, u32[]{:S(2)}, u32[]{:S(2)}) collective-permute-start(bf16[512,8,128]{2,0,1:T(8,128)(2,1)} %copy.71), channel_id=1, source_target_pairs={{0,2},{2,4},{4,6},{6,8},{8,10},{10,12},{12,14},{14,16},{16,18},{18... | collective-permute-start | bytes 3145736 | tf_op jit(solution)/shard_map/ppermute | solution.py:13
  16.5 3.4 %collective-permute-start.2 = (bf16[512,8,128]{2,0,1:T(8,128)(2,1)}, bf16[512,8,128]{2,0,1:T(8,128)(2,1)}, u32[]{:S(2)}, u32[]{:S(2)}) collective-permute-start(bf16[512,8,128]{2,0,1:T(8,128)(2,1)} %copy.71), channel_id=1, source_target_pairs={{0,4},{2,6},{4,8},{6,10},{8,12},{10,14},{12,16},{14,18},{16,20},{1... | collective-permute-start | bytes 3145736 | tf_op jit(solution)/shard_map/ppermute | solution.py:13
  20.1 2.6 convert_element_type.31
  23.7 10.1 %fusion.48 = f32[8,512,512,2]{2,1,3,0:T(8,128)} fusion(bf16[512,8,128]{2,0,1:T(8,128)(2,1)} %copy.71, bf16[512,8,2,128]{3,2,1,0:T(2,128)(2,1)S(1)} %bitcast.144), kind=kOutput, calls=%fused_computation.53 | convolution fusion | flops 1073741824 | bytes 19922944 | tf_op jit(solution)/shard_map/tkgd,skd->kgts/dot_general | solution.py:20
  33.9 11.4 %fusion.9 = bf16[8,2,512,512]{2,3,1,0:T(8,128)(2,1)} fusion(f32[8,512,512,2]{2,1,3,0:T(8,128)} %fusion.48, f32[8,2,512]{2,1,0:T(2,128)S(1)} %sub.57, f32[8,2,512]{2,1,0:T(2,128)S(1)} %sub.54, pred[512,512]{0,1:T(8,128)(4,1)S(1)} %fusion.57, bf16[512,8,128]{2,0,1:T(8,128)(2,1)} %copy.70, bf16[512,8,2,128]{3,2,1,0:T(2,128)(2,1)S(1)} %bitcast.151), kind=kOutput, calls=%fused_computation.14 | convolution fusion | flops 1098907648 | bytes 28639232 | tf_op jit(solution)/shard_map/tkgd,skd->kgts/dot_general | solution.py:26
  46.2 6.3 %fusion.46 = f32[8,2,512,128]{3,2,1,0:T(8,128)S(1)} fusion(bf16[8,2,512,512]{2,3,1,0:T(8,128)(2,1)} %fusion.9, bf16[512,8,128]{2,0,1:T(8,128)(2,1)} %copy.71), kind=kOutput, calls=%fused_computation.51 | convolution fusion | flops 1073741824 | bytes 13631488 | tf_op jit(solution)/shard_map/kgts,skd->tkgd/dot_general | solution.py:33
  52.9 9.5 %fusion.43 = f32[8,512,512,2]{2,1,3,0:T(8,128)} fusion(bf16[512,8,128]{2,0,1:T(8,128)(2,1)} %collective-permute-done, bf16[512,8,2,128]{3,2,1,0:T(2,128)(2,1)S(1)} %bitcast.145), kind=kOutput, calls=%fused_computation.48 | convolution fusion | flops 1073741824 | bytes 19922944 | tf_op jit(solution)/shard_map/tkgd,skd->kgts/dot_general | solution.py:20
  62.4 11.4 %fusion.5 = bf16[8,2,512,512]{2,3,1,0:T(8,128)(2,1)} fusion(f32[8,512,512,2]{2,1,3,0:T(8,128)} %fusion.43, f32[8,2,512]{2,1,0:T(2,128)S(1)} %sub.57, f32[8,2,512]{2,1,0:T(2,128)S(1)} %sub.54, pred[512,512]{0,1:T(8,128)(4,1)S(1)} %fusion.59, bf16[512,8,128]{2,0,1:T(8,128)(2,1)} %collective-permute-done.1, bf16[512,8,2,128]{3,2,1,0:T(2,128)(2,1)S(1)} %bitcast.155), kind=kOutput, calls=%fused_computation.8 | convolution fusion | flops 1098907648 | bytes 28639232 | tf_op jit(solution)/shard_map/tkgd,skd->kgts/dot_general | solution.py:26
  73.8 11.1 %fusion.30 = f32[512,8,128]{2,0,1:T(8,128)} fusion(f32[8,512,512,2]{2,1,3,0:T(8,128)} %fusion.43, f32[8,2,512]{2,1,0:T(2,128)S(1)} %sub.54, pred[512,512]{0,1:T(8,128)(4,1)} %copy-done.7, bf16[512,8,2,128]{3,2,1,0:T(2,128)(2,1)} %bitcast.152), kind=kOutput, calls=%fused_computation.39 | convolution fusion | flops 1090519040 | bytes 21266432 | tf_op jit(solution)/shard_map/kgts,tkgd->skd/dot_general | solution.py:38
  84.9 7.1 %fusion.26 = f32[512,8,128]{2,0,1:T(8,128)} fusion(bf16[8,2,512,512]{2,3,1,0:T(8,128)(2,1)} %fusion.5, bf16[512,8,2,128]{3,2,1,0:T(2,128)(2,1)S(1)} %bitcast.146), kind=kOutput, calls=%fused_computation.33 | convolution fusion | flops 1074266112 | bytes 12582912 | tf_op jit(solution)/shard_map/kgts,tkgd->skd/dot_general | solution.py:39
  93.4 9.3 %fusion.38 = f32[8,512,512,2]{2,1,3,0:T(8,128)} fusion(bf16[512,8,128]{2,0,1:T(8,128)(2,1)} %collective-permute-done.2, bf16[512,8,2,128]{3,2,1,0:T(2,128)(2,1)S(1)} %bitcast.147), kind=kOutput, calls=%fused_computation.43 | convolution fusion | flops 1073741824 | bytes 19922944 | tf_op jit(solution)/shard_map/tkgd,skd->kgts/dot_general | solution.py:20
  102.8 10.2 %fusion.1 = bf16[8,2,512,512]{2,3,1,0:T(8,128)(2,1)S(1)} fusion(f32[8,512,512,2]{2,1,3,0:T(8,128)} %fusion.38, f32[8,2,512]{2,1,0:T(2,128)S(1)} %sub.57, f32[8,2,512]{2,1,0:T(2,128)S(1)} %sub.54, pred[512,512]{0,1:T(8,128)(4,1)S(1)} %copy-done.6, bf16[512,8,128]{2,0,1:T(8,128)(2,1)} %collective-permute-done.3, bf16[512,8,2,128]{3,2,1,0:T(2,128)(2,1)} %bitcast.153), kind=kOutput, calls=%fused_computation.2 | convolution fusion | flops 1098907648 | bytes 28639232 | tf_op jit(solution)/shard_map/tkgd,skd->kgts/dot_general | solution.py:26
  113.0 4.1 %fusion.25 = f32[512,8,128]{2,0,1:T(8,128)} fusion(bf16[8,2,512,512]{2,3,1,0:T(8,128)(2,1)S(1)} %fusion.1, bf16[512,8,2,128]{3,2,1,0:T(2,128)(2,1)S(1)} %bitcast.148), kind=kOutput, calls=%fused_computation.31 | convolution fusion | flops 1074266112 | bytes 12582912 | tf_op jit(solution)/shard_map/kgts,tkgd->skd/dot_general | solution.py:39
  118.4 11.0 %fusion.33 = f32[512,8,128]{2,0,1:T(8,128)} fusion(f32[8,512,512,2]{2,1,3,0:T(8,128)} %fusion.38, f32[8,2,512]{2,1,0:T(2,128)S(1)} %sub.54, pred[512,512]{0,1:T(8,128)(4,1)} %fusion.61, bf16[512,8,2,128]{3,2,1,0:T(2,128)(2,1)} %bitcast.154), kind=kOutput, calls=%fused_computation.40 | convolution fusion | flops 1090519040 | bytes 21266432 | tf_op jit(solution)/shard_map/kgts,tkgd->skd/dot_general | solution.py:38
  132.2 8.3 %fusion.41 = f32[8,2,512,128]{3,2,1,0:T(8,128)} fusion(bf16[8,2,512,512]{2,3,1,0:T(8,128)(2,1)} %fusion.5, bf16[512,8,128]{2,0,1:T(8,128)(2,1)} %collective-permute-done), kind=kOutput, calls=%fused_computation.46 | convolution fusion | flops 1073741824 | bytes 13631488 | tf_op jit(solution)/shard_map/kgts,skd->tkgd/dot_general | solution.py:33
  140.5 9.8 %add_multiply_fusion = f32[8,2,512,128]{3,2,1,0:T(8,128)} fusion(f32[8,2,512,128]{3,2,1,0:T(8,128)S(1)} %fusion.46, f32[8,2,512,128]{3,2,1,0:T(8,128)} %fusion.41, bf16[8,2,512,512]{2,3,1,0:T(8,128)(2,1)} %copy-done, bf16[512,8,128]{2,0,1:T(8,128)(2,1)} %collective-permute-done.2), kind=kOutput, calls=%fused_computation.27 | convolution fusion | flops 1076887552 | bytes 22020096 | tf_op jit(solution)/shard_map/kgts,skd->tkgd/dot_general | solution.py:33
  150.2 6.6 %copy.26 = f32[512,16,128]{2,1,0:T(8,128)} copy(f32[512,16,128]{2,0,1:T(8,128)} %bitcast.150) | data formatting | bytes 8388608
  156.9 24.0 %collective-permute-done.5 = f32[512,8,128]{2,0,1:T(8,128)} collective-permute-done((f32[512,8,128]{2,0,1:T(8,128)}, f32[512,8,128]{2,0,1:T(8,128)}, u32[]{:S(2)}, u32[]{:S(2)}) %collective-permute-start.5) | collective-permute-done | bytes 2097184 | tf_op jit(solution)/shard_map/ppermute | solution.py:13
  180.9 7.0 %fusion.27 = f32[512,8,128]{2,0,1:T(8,128)S(1)} fusion(f32[512,8,128]{2,0,1:T(8,128)} %collective-permute-done.5, f32[512,8,128]{2,0,1:T(8,128)} %collective-permute-done.4, bf16[8,2,512,512]{2,3,1,0:T(8,128)(2,1)} %fusion.9, bf16[512,8,2,128]{3,2,1,0:T(2,128)(2,1)S(1)} %bitcast.149), kind=kOutput, calls=%fused_computation.35 | convolution fusion | flops 1075314688 | bytes 16777216 | tf_op jit(solution)/shard_map/kgts,tkgd->skd/dot_general | solution.py:39
  190.5 57.7 %collective-permute-done.7 = f32[512,8,128]{2,0,1:T(8,128)} collective-permute-done((f32[512,8,128]{2,0,1:T(8,128)}, f32[512,8,128]{2,0,1:T(8,128)}, u32[]{:S(2)}, u32[]{:S(2)}) %collective-permute-start.7) | collective-permute-done | bytes 2097184 | tf_op jit(solution)/shard_map/ppermute | solution.py:13
  248.1 10.6 %fusion.24 = f32[512,8,128]{2,0,1:T(8,128)} fusion(f32[512,8,128]{2,0,1:T(8,128)} %collective-permute-done.7, f32[512,8,128]{2,0,1:T(8,128)} %collective-permute-done.6, f32[8,512,512,2]{2,1,3,0:T(8,128)} %fusion.48, f32[8,2,512]{2,1,0:T(2,128)S(1)} %sub.54, pred[512,512]{0,1:T(8,128)(4,1)S(1)} %fusion.57, bf16[512,8,2,128]{3,2,1,0:T(2,128)(2,1)S(1)} %bitcast.156), kind=kOutput, calls=%fused_computation.29 | convolution fusion | flops 1091567616 | bytes 25460736 | tf_op jit(solution)/shard_map/kgts,tkgd->skd/dot_general | solution.py:38
  258.8 4.1 %copy.28 = f32[512,8,128]{2,1,0:T(8,128)} copy(f32[512,8,128]{2,0,1:T(8,128)} %fusion.24) | data formatting | bytes 4194304
  (41 shorter events, 14.2 us)
Async XLA Ops:
  0.6 11.4 %copy-start.5 = (f32[512,8,128]{2,1,0:T(8,128)S(1)}, f32[512,8,128]{2,1,0:T(8,128)}, u32[]{:S(2)}) copy-start(f32[512,8,128]{2,1,0:T(8,128)} %param.7) | copy-start | bytes 6291460
  0.6 19.3 %copy-start.8 = (f32[16,512]{1,0:T(8,128)S(1)}, f32[16,512]{1,0:T(8,128)}, u32[]{:S(2)}) copy-start(f32[16,512]{1,0:T(8,128)} %param.10) | copy-start | bytes 98308
  0.7 19.3 %copy-start.9 = (f32[16,512]{1,0:T(8,128)S(1)}, f32[16,512]{1,0:T(8,128)}, u32[]{:S(2)}) copy-start(f32[16,512]{1,0:T(8,128)} %param.11) | copy-start | bytes 98308
  3.8 99.0 %collective-permute-start.3 = (bf16[512,8,128]{2,0,1:T(8,128)(2,1)}, bf16[512,8,128]{2,0,1:T(8,128)(2,1)}, u32[]{:S(2)}, u32[]{:S(2)}) collective-permute-start(bf16[512,8,128]{2,0,1:T(8,128)(2,1)} %copy.70), channel_id=1, source_target_pairs={{0,4},{2,6},{4,8},{6,10},{8,12},{10,14},{12,16},{14,18},{16,20},{1... | collective-permute-start | bytes 3145736 | tf_op jit(solution)/shard_map/ppermute | solution.py:13
  9.6 52.8 %collective-permute-start.1 = (bf16[512,8,128]{2,0,1:T(8,128)(2,1)}, bf16[512,8,128]{2,0,1:T(8,128)(2,1)}, u32[]{:S(2)}, u32[]{:S(2)}) collective-permute-start(bf16[512,8,128]{2,0,1:T(8,128)(2,1)} %copy.70), channel_id=1, source_target_pairs={{0,2},{2,4},{4,6},{6,8},{8,10},{10,12},{12,14},{14,16},{16,18},{18... | collective-permute-start | bytes 3145736 | tf_op jit(solution)/shard_map/ppermute | solution.py:13
  13.4 39.4 %collective-permute-start = (bf16[512,8,128]{2,0,1:T(8,128)(2,1)}, bf16[512,8,128]{2,0,1:T(8,128)(2,1)}, u32[]{:S(2)}, u32[]{:S(2)}) collective-permute-start(bf16[512,8,128]{2,0,1:T(8,128)(2,1)} %copy.71), channel_id=1, source_target_pairs={{0,2},{2,4},{4,6},{6,8},{8,10},{10,12},{12,14},{14,16},{16,18},{18... | collective-permute-start | bytes 3145736 | tf_op jit(solution)/shard_map/ppermute | solution.py:13
  16.5 76.9 %collective-permute-start.2 = (bf16[512,8,128]{2,0,1:T(8,128)(2,1)}, bf16[512,8,128]{2,0,1:T(8,128)(2,1)}, u32[]{:S(2)}, u32[]{:S(2)}) collective-permute-start(bf16[512,8,128]{2,0,1:T(8,128)(2,1)} %copy.71), channel_id=1, source_target_pairs={{0,4},{2,6},{4,8},{6,10},{8,12},{10,14},{12,16},{14,18},{16,20},{1... | collective-permute-start | bytes 3145736 | tf_op jit(solution)/shard_map/ppermute | solution.py:13
  20.0 3.5 %copy-start.1 = (f32[512,16,128]{2,1,0:T(8,128)S(1)}, f32[512,16,128]{2,1,0:T(8,128)}, u32[]{:S(2)}) copy-start(f32[512,16,128]{2,1,0:T(8,128)} %param.9) | copy-start | bytes 12582916
  23.7 10.1 %copy-start.2 = (bf16[512,16,128]{2,1,0:T(8,128)(2,1)}, bf16[512,16,128]{2,1,0:T(8,128)(2,1)S(1)}, u32[]{:S(2)}) copy-start(bf16[512,16,128]{2,1,0:T(8,128)(2,1)S(1)} %convert_element_type.33) | copy-start | bytes 6291460
  52.8 9.5 %copy-start.7 = (pred[512,512]{0,1:T(8,128)(4,1)}, pred[512,512]{0,1:T(8,128)(4,1)S(1)}, u32[]{:S(2)}) copy-start(pred[512,512]{0,1:T(8,128)(4,1)S(1)} %fusion.59) | copy-start | bytes 786436
  52.9 9.5 %copy-start.3 = (bf16[512,16,128]{2,1,0:T(8,128)(2,1)S(1)}, bf16[512,16,128]{2,1,0:T(8,128)(2,1)}, u32[]{:S(2)}) copy-start(bf16[512,16,128]{2,1,0:T(8,128)(2,1)} %copy-done.2) | copy-start | bytes 6291460
  92.0 10.8 %copy-start.6 = (pred[512,512]{0,1:T(8,128)(4,1)S(1)}, pred[512,512]{0,1:T(8,128)(4,1)}, u32[]{:S(2)}) copy-start(pred[512,512]{0,1:T(8,128)(4,1)} %fusion.61) | copy-start | bytes 786436
  92.0 64.9 %collective-permute-start.4 = (f32[512,8,128]{2,0,1:T(8,128)}, f32[512,8,128]{2,0,1:T(8,128)}, u32[]{:S(2)}, u32[]{:S(2)}) collective-permute-start(f32[512,8,128]{2,0,1:T(8,128)} %fusion.26), channel_id=1, source_target_pairs={{2,0},{4,2},{6,4},{8,6},{10,8},{12,10},{14,12},{16,14},{18,16},{20... | collective-permute-start | bytes 6291464 | tf_op jit(solution)/shard_map/ppermute | solution.py:13
  113.0 4.1 %copy-start = (bf16[8,2,512,512]{2,3,1,0:T(8,128)(2,1)}, bf16[8,2,512,512]{2,3,1,0:T(8,128)(2,1)S(1)}, u32[]{:S(2)}) copy-start(bf16[8,2,512,512]{2,3,1,0:T(8,128)(2,1)S(1)} %fusion.1) | copy-start | bytes 25165828
  117.1 63.8 %collective-permute-start.5 = (f32[512,8,128]{2,0,1:T(8,128)}, f32[512,8,128]{2,0,1:T(8,128)}, u32[]{:S(2)}, u32[]{:S(2)}) collective-permute-start(f32[512,8,128]{2,0,1:T(8,128)} %fusion.25), channel_id=1, source_target_pairs={{4,0},{6,2},{8,4},{10,6},{12,8},{14,10},{16,12},{18,14},{20,16},{2... | collective-permute-start | bytes 6291464 | tf_op jit(solution)/shard_map/ppermute | solution.py:13
  129.4 61.1 %collective-permute-start.6 = (f32[512,8,128]{2,0,1:T(8,128)}, f32[512,8,128]{2,0,1:T(8,128)}, u32[]{:S(2)}, u32[]{:S(2)}) collective-permute-start(f32[512,8,128]{2,0,1:T(8,128)} %fusion.30), channel_id=1, source_target_pairs={{2,0},{4,2},{6,4},{8,6},{10,8},{12,10},{14,12},{16,14},{18,16},{20... | collective-permute-start | bytes 6291464 | tf_op jit(solution)/shard_map/ppermute | solution.py:13
  130.7 117.5 %collective-permute-start.7 = (f32[512,8,128]{2,0,1:T(8,128)}, f32[512,8,128]{2,0,1:T(8,128)}, u32[]{:S(2)}, u32[]{:S(2)}) collective-permute-start(f32[512,8,128]{2,0,1:T(8,128)} %fusion.33), channel_id=1, source_target_pairs={{4,0},{6,2},{8,4},{10,6},{12,8},{14,10},{16,12},{18,14},{20,16},{2... | collective-permute-start | bytes 6291464 | tf_op jit(solution)/shard_map/ppermute | solution.py:13
  187.9 60.2 %copy-start.4 = (bf16[512,16,128]{2,1,0:T(8,128)(2,1)S(1)}, bf16[512,16,128]{2,1,0:T(8,128)(2,1)}, u32[]{:S(2)}) copy-start(bf16[512,16,128]{2,1,0:T(8,128)(2,1)} %copy-done.2) | copy-start | bytes 6291460
where the time goes:
time: 267 us; the launch traced here: 263 us
  matrix products  137 us (51%)
  waiting for transfers between devices  81.7 us (31%)
  starting transfers between devices  20.2 us (8%)
  local copies, waits for them, and re-layouts  18.6 us (7%)
  other arithmetic  4.27 us (2%)
    ppermute x8, waiting for transfers between devices, shifted(): return lax.ppermute(x, axis, pairs)  81.7 us
    dot_general x3, matrix products, probe(): jnp.einsum('tkgd,skd->kgts', gradient_list, values, preferred_element_typ...  33 us
    dot_general x3, matrix products, owner_terms(): jnp.einsum('kgts,tkgd->skd', probs, gradient_list, preferred_element_type...  32.7 us
    dot_general x3, matrix products, probe(): jnp.einsum('tkgd,skd->kgts', query_rows, keys, preferred_element_type=jnp...  29 us
    dot_general x3, matrix products, query_term(): jnp.einsum('kgts,skd->tkgd', dscore, keys, preferred_element_type=jnp.flo...  24.4 us
    ppermute x8, starting transfers between devices, shifted(): return lax.ppermute(x, axis, pairs)  20.2 us
    unnamed x25, local copies, waits for them, and re-layouts  18.5 us
    dot_general x3, matrix products, owner_terms(): jnp.einsum('kgts,tkgd->skd', dscore, query_rows, preferred_element_type=j...  18.1 us
  transfers between devices with their start and end apart: 8, of which 2 were waited for; matrix products, arithmetic and copies ran while one was open for 54% of the time, Pallas kernels for 0%

commit v1 on v0

v1 whole, which is shorter than its diff:
```python
import functools
import math

import jax
import jax.numpy as jnp
from jax import lax
from jax.experimental import pallas as pl
from jax.experimental.pallas import tpu as pltpu
from jax.sharding import PartitionSpec as P

WINDOW = 1024
QSCALE = 168
SCALE = QSCALE ** (-0.5)
LOG2E = math.log2(math.e)
MESH = pl.DeviceIdType.MESH
BF16 = jnp.bfloat16
F32 = jnp.float32


def dot(a, b, ca, cb):
    return lax.dot_general(a, b, (((ca,), (cb,)), ((), ())), preferred_element_type=F32)


def kernel(
    tokens, kheads, group, devices,
    q_hbm, k_hbm, v_hbm, g_hbm, lse_ref, dots_ref,
    dq_hbm, dk_ref, dv_ref,
    q_ref, k_ref, v_ref, g_ref, dq_ref,
    own, far, near, gnear_out, gnear_in, gfar_out, gfar_in,
    held, dq_acc, qb, gb,
    load_sem, store_sem,
    far_send, far_recv, near_send, near_recv,
    gnear_send, gnear_recv, gfar_send, gfar_recv,
):
    qheads = kheads * group
    half = tokens // 2
    me = lax.axis_index("seq")
    core = lax.rem(me, 2)
    partner = me + 1 - 2 * core
    has_far = me >= 2
    has_near = me >= 1
    has_next = me + 2 < devices
    gets_near = jnp.logical_or(core == 0, has_far)

    loads = [
        pltpu.make_async_copy(src, dst, load_sem.at[n])
        for n, (src, dst) in enumerate(
            ((k_hbm, k_ref), (v_hbm, v_ref), (q_hbm, q_ref), (g_hbm, g_ref))
        )
    ]
    for load in loads:
        load.start()

    barrier = pltpu.get_barrier_semaphore()
    pl.semaphore_signal(barrier, inc=1, device_id={"seq": partner}, device_id_type=MESH)

    @pl.when(has_far)
    def _():
        pl.semaphore_signal(barrier, inc=1, device_id={"seq": me - 2}, device_id_type=MESH)

    @pl.when(has_next)
    def _():
        pl.semaphore_signal(barrier, inc=1, device_id={"seq": me + 2}, device_id_type=MESH)

    pl.semaphore_wait(barrier, 1 + has_far.astype(jnp.int32) + has_next.astype(jnp.int32))

    def remote(src, dst, send, recv, h, to):
        return pltpu.make_async_remote_copy(
            src_ref=src.at[h], dst_ref=dst.at[h], send_sem=send.at[h], recv_sem=recv.at[h],
            device_id={"seq": to}, device_id_type=MESH,
        )

    def far_copy(h):
        return remote(own, far, far_send, far_recv, h, me + 2)

    def near_own(h):
        return remote(own, near, near_send, near_recv, h, partner)

    def near_relay(h):
        return remote(far, near, near_send, near_recv, h, partner)

    def gnear_copy(h):
        return remote(gnear_out, gnear_in, gnear_send, gnear_recv, h, partner)

    def gfar_copy(h):
        return remote(gfar_out, gfar_in, gfar_send, gfar_recv, h, me - 2)

    loads[0].wait()
    loads[1].wait()

    def send_own(h, _):
        own[h, 0:tokens] = k_ref[pl.ds(h, tokens, stride=kheads), :].astype(BF16)
        own[h, tokens:] = v_ref[pl.ds(h, tokens, stride=kheads), :].astype(BF16)

        @pl.when(has_next)
        def _():
            far_copy(h).start()

        @pl.when(core == 0)
        def _():
            near_own(h).start()

        return 0

    lax.fori_loop(0, kheads, send_own, 0)
    loads[2].wait()
    loads[3].wait()

    def block(kind, h, kv, emit):
        for jb in range(2):
            k = kv[h, jb * half:(jb + 1) * half]
            v = kv[h, tokens + jb * half:tokens + (jb + 1) * half]
            dk = dv = None
            for g in range(group):
                lo, hi = 0, tokens
                if kind == "own":
                    lo = jb * half
                elif kind == "far":
                    hi = (jb + 1) * half
                rows = slice(g * tokens + lo, g * tokens + hi)
                q = qb[rows]
                go = gb[rows]
                lse = lse_ref[pl.ds(h * group + g, 1), lo:hi]
                dots = dots_ref[pl.ds(h * group + g, 1), lo:hi]
                s = dot(k, q, 1, 1)
                p = jnp.exp2(s * (SCALE * LOG2E) - lse * LOG2E)
                if kind != "near":
                    kpos = lax.broadcasted_iota(jnp.int32, p.shape, 0) + jb * half
                    qpos = lax.broadcasted_iota(jnp.int32, p.shape, 1) + lo
                    keep = qpos >= kpos if kind == "own" else qpos < kpos
                    p = jnp.where(keep, p, 0.0)
                ds = (p * (dot(v, go, 1, 1) - dots)).astype(BF16)
                dv_term = dot(p.astype(BF16), go, 1, 0)
                dk_term = dot(ds, q, 1, 0)
                dv = dv_term if dv is None else dv + dv_term
                dk = dk_term if dk is None else dk + dk_term
                dq = dot(ds, k, 0, 0)
                if kind == "own" and jb == 0:
                    dq_acc[rows] = dq
                else:
                    dq_acc[rows] += dq
            emit(jb, dk * SCALE, dv)

    def send_sum(h):
        slot = lax.rem(h, 2)
        gnear_copy(h).wait_recv()
        gfar_out[h] = (held[slot] + gnear_in[h].astype(F32)).astype(BF16)
        gfar_copy(h).start()

    def step(h, _):
        @pl.when(jnp.logical_and(core == 1, has_far))
        def _():
            far_copy(h).wait_recv()
            near_relay(h).start()

        for g in range(group):
            rows = slice(g * tokens, (g + 1) * tokens)
            at = pl.ds(h * group + g, tokens, stride=qheads)
            qb[rows] = q_ref[at, :].astype(BF16)
            gb[rows] = g_ref[at, :].astype(BF16)

        def emit_own(jb, dk, dv):
            at = pl.ds(jb * half * kheads + h, half, stride=kheads)
            dk_ref[at, :] = dk
            dv_ref[at, :] = dv

        block("own", h, own, emit_own)

        @pl.when(has_near)
        def _():
            jax.lax.cond(
                core == 0,
                lambda: near_relay(h).wait_recv(),
                lambda: near_own(h).wait_recv(),
            )

            def emit_near(jb, dk, dv):
                gnear_out[h, jb * half:(jb + 1) * half] = dk.astype(BF16)
                gnear_out[h, tokens + jb * half:tokens + (jb + 1) * half] = dv.astype(BF16)

            block("near", h, near, emit_near)
            gnear_copy(h).start()

        @pl.when(has_far)
        def _():
            @pl.when(core == 0)
            def _():
                far_copy(h).wait_recv()

            slot = lax.rem(h, 2)

            @pl.when(jnp.logical_and(core == 1, h >= 1))
            def _():
                send_sum(h - 1)

            def emit_far(jb, dk, dv):
                held[slot, jb * half:(jb + 1) * half] = dk
                held[slot, tokens + jb * half:tokens + (jb + 1) * half] = dv

            block("far", h, far, emit_far)

            @pl.when(core == 0)
            def _():
                gfar_out[h] = held[slot].astype(BF16)
                gfar_copy(h).start()

        for g in range(group):
            at = pl.ds(h * group + g, tokens, stride=qheads)
            dq_ref[at, :] = dq_acc[g * tokens:(g + 1) * tokens] * SCALE
        return 0

    lax.fori_loop(0, kheads, step, 0)

    @pl.when(jnp.logical_and(core == 1, has_far))
    def _():
        send_sum(kheads - 1)

    store = pltpu.make_async_copy(dq_ref, dq_hbm, store_sem)
    store.start()

    def finish(h, _):
        at = pl.ds(h, tokens, stride=kheads)

        @pl.when(core == 0)
        def _():
            gnear_copy(h).wait_recv()
            dk_ref[at, :] += gnear_in[h, 0:tokens].astype(F32)
            dv_ref[at, :] += gnear_in[h, tokens:].astype(F32)

        @pl.when(has_next)
        def _():
            gfar_copy(h).wait_recv()
            dk_ref[at, :] += gfar_in[h, 0:tokens].astype(F32)
            dv_ref[at, :] += gfar_in[h, tokens:].astype(F32)

        return 0

    lax.fori_loop(0, kheads, finish, 0)

    def drain(h, _):
        @pl.when(has_next)
        def _():
            far_copy(h).wait_send()

        @pl.when(gets_near)
        def _():
            near_own(h).wait_send()

        @pl.when(has_near)
        def _():
            gnear_copy(h).wait_send()

        @pl.when(has_far)
        def _():
            gfar_copy(h).wait_send()

        return 0

    lax.fori_loop(0, kheads, drain, 0)
    store.wait()


def on_device(devices, query, key, value, gradient, logsumexp, dots):
    tokens, qheads, width = query.shape
    kheads = key.shape[1]
    group = qheads // kheads
    assert WINDOW == 2 * tokens
    flat_q = (tokens * qheads, width)
    flat_k = (tokens * kheads, width)
    message = pltpu.VMEM((kheads, 2 * tokens, width), BF16)
    anywhere = pl.BlockSpec(memory_space=pl.ANY)
    vmem = pl.BlockSpec(memory_space=pltpu.VMEM)
    sems = pltpu.SemaphoreType.DMA((kheads,))
    dq, dk, dv = pl.pallas_call(
        functools.partial(kernel, tokens, kheads, group, devices),
        out_shape=(
            jax.ShapeDtypeStruct(flat_q, F32),
            jax.ShapeDtypeStruct(flat_k, F32),
            jax.ShapeDtypeStruct(flat_k, F32),
        ),
        in_specs=[anywhere] * 4 + [vmem] * 2,
        out_specs=(anywhere, vmem, vmem),
        scratch_shapes=[
            pltpu.VMEM(flat_q, F32),
            pltpu.VMEM(flat_k, F32),
            pltpu.VMEM(flat_k, F32),
            pltpu.VMEM(flat_q, F32),
            pltpu.VMEM(flat_q, F32),
        ] + [message] * 7 + [
            pltpu.VMEM((2, 2 * tokens, width), F32),
            pltpu.VMEM((group * tokens, width), F32),
            pltpu.VMEM((group * tokens, width), BF16),
            pltpu.VMEM((group * tokens, width), BF16),
            pltpu.SemaphoreType.DMA((4,)),
            pltpu.SemaphoreType.DMA,
        ] + [sems] * 8,
        compiler_params=pltpu.CompilerParams(
            collective_id=0, has_side_effects=True, vmem_limit_bytes=58 * 2**20
        ),
        cost_estimate=pl.CostEstimate(
            flops=10 * qheads * tokens * WINDOW * width,
            bytes_accessed=(3 * qheads + 4 * kheads) * tokens * width * 4,
            transcendentals=qheads * tokens * WINDOW,
        ),
    )(
        query.reshape(flat_q), key.reshape(flat_k), value.reshape(flat_k),
        gradient.reshape(flat_q), logsumexp, dots,
    )
    return dq.reshape(query.shape), dk.reshape(key.shape), dv.reshape(value.shape)


def solution(mesh):
    return jax.shard_map(
        functools.partial(on_device, mesh.shape["seq"]),
        mesh=mesh,
        in_specs=(
            P("seq", "head", None),
            P("seq", "head", None),
            P("seq", "head", None),
            P("seq", "head", None),
            P("head", "seq"),
            P("head", "seq"),
        ),
        out_specs=(P("seq", "head", None), P("seq", "head", None), P("seq", "head", None)),
        check_vma=False,
    )
```

time: 267 us -> 121 us (0.45); the launches traced: 263 us -> 120 us
  matrix products: 137 us -> 0 us
  Pallas kernels: 0 us -> 111 us
  waiting for transfers between devices: 81.7 us -> 0 us
  starting transfers between devices: 20.2 us -> 0 us
  local copies, waits for them, and re-layouts: 18.6 us -> 8.29 us
  other arithmetic: 4.27 us -> 0 us
    dot_general x15 -> x0, matrix products: 137 us -> none  [the longest x3 33 us: probe(): jnp.einsum('tkgd,skd->kgts', gradient_list, values, preferred_element_typ...]
    pallas_call x0 -> x1, Pallas kernels: none -> 111 us  [on_device(): pl.pallas_call(functools.partial(kernel, tokens, kheads, group, devices),...]
    ppermute x8 -> x0, waiting for transfers between devices: 81.7 us -> none  [shifted(): return lax.ppermute(x, axis, pairs)]
    ppermute x8 -> x0, starting transfers between devices: 20.2 us -> none  [shifted(): return lax.ppermute(x, axis, pairs)]
    unnamed x25 -> x7, local copies, waits for them, and re-layouts: 18.5 us -> 8.29 us
    convert_element_type x2 -> x0, other arithmetic: 2.9 us -> none  [the longest x1 2.62 us: on_device(): query_tensor.astype(jnp.bfloat16)]
  transfers between devices with their start and end apart: 8 -> 0, of which waited for: 2 -> 0; matrix products, arithmetic and copies ran while one was open for 54% -> 0% of each run, Pallas kernels for 0% -> 0%
where the time goes in v1:
time: 121 us; the launch traced here: 120 us
  Pallas kernels  111 us (92%)
  local copies, waits for them, and re-layouts  8.29 us (7%)
    pallas_call x1, Pallas kernels, on_device(): pl.pallas_call(functools.partial(kernel, tokens, kheads, group, devices),...  111 us
    unnamed x7, local copies, waits for them, and re-layouts  8.29 us

profile of v1, /device:TPU:0, one launch (start us, length us, event | category | flops | bytes accessed | tf_op | source)
XLA Modules:
  0.0 119.8 jit_solution(10466783677828996444)
XLA Ops:
  0.6 110.9 %shard_map.85 = (f32[8192,128]{1,0:T(8,128)}, f32[4096,128]{1,0:T(8,128)}, f32[4096,128]{1,0:T(8,128)}) custom-call(f32[8192,128]{1,0:T(8,128)} %bitcast.10, f32[4096,128]{1,0:T(8,128)} %bitcast.12, f32[4096,128]{1,0:T(8,128)} %bitcast.13, f32[8192,128]{1,0:T(8,128)} %bitcast.11, f32[16,512]{1,0:T(8,128)} %lse_ref.1, f32[16,512]{1,0:T(8,128)} %dots_ref.1), custom_call_target="tpu_custom_call" | custom-call | flops 10737418240 | bytes 20971520 | tf_op jit(solution)/shard_map/pallas_call | solution.py:274
  111.5 0.0 copy-start.1
  111.5 4.6 %copy.12 = f32[512,16,128]{2,1,0:T(8,128)} copy(f32[512,16,128]{2,1,0:T(8,128)} %bitcast.7) | data formatting | bytes 8388608
  116.1 0.0 copy-done.1
  116.1 0.0 copy-start
  116.1 1.3 %copy.13 = f32[512,8,128]{2,1,0:T(8,128)} copy(f32[512,8,128]{2,1,0:T(8,128)S(1)} %bitcast.9) | data formatting | bytes 4194304
  117.4 1.0 copy-done
  118.5 1.3 %copy.14 = f32[512,8,128]{2,1,0:T(8,128)} copy(f32[512,8,128]{2,1,0:T(8,128)S(1)} %bitcast.8) | data formatting | bytes 4194304
Async XLA Ops:
  111.5 4.6 %copy-start.1 = (f32[4096,128]{1,0:T(8,128)S(1)}, f32[4096,128]{1,0:T(8,128)}, u32[]{:S(2)}) copy-start(f32[4096,128]{1,0:T(8,128)} %get-tuple-element.7) | copy-start | bytes 6291460
  116.1 2.3 %copy-start = (f32[4096,128]{1,0:T(8,128)S(1)}, f32[4096,128]{1,0:T(8,128)}, u32[]{:S(2)}) copy-start(f32[4096,128]{1,0:T(8,128)} %get-tuple-element.8) | copy-start | bytes 6291460

commit v2 on v1

--- a/solution.py
+++ b/solution.py
@@ -26,11 +26,11 @@
     q_hbm, k_hbm, v_hbm, g_hbm, lse_ref, dots_ref,
     dq_hbm, dk_ref, dv_ref,
     q_ref, k_ref, v_ref, g_ref, dq_ref,
-    own, far, near, gnear_out, gnear_in, gfar_out, gfar_in,
+    own, far, near, relay, gnear_out, gnear_in, gfar_out, gfar_in,
     held, dq_acc, qb, gb,
     load_sem, store_sem,
     far_send, far_recv, near_send, near_recv,
-    gnear_send, gnear_recv, gfar_send, gfar_recv,
+    gnear_send, gnear_recv, gfar_send, gfar_recv, relay_send, relay_recv,
 ):
     qheads = kheads * group
     half = tokens // 2
@@ -41,6 +41,27 @@
     has_near = me >= 1
     has_next = me + 2 < devices
     gets_near = jnp.logical_or(core == 0, has_far)
+    pairs = devices // 4
+    pair = me // 4
+    odd = lax.rem(me // 2, 2) == 1
+
+    def picked(h, share):
+        return lax.rem(h * share, pairs) < share
+
+    def both(*terms):
+        return functools.reduce(jnp.logical_and, terms)
+
+    def detours_forward(h):
+        return both(odd, has_next, picked(h + 3, pair + 1))
+
+    def relays_forward(h):
+        return both(odd, pair >= 1, picked(h + 3, pair))
+
+    def detours_back(h):
+        return both(jnp.logical_not(odd), pair >= 1, picked(h, pairs - pair))
+
+    def relays_back(h):
+        return both(jnp.logical_not(odd), pair + 1 < pairs, picked(h, pairs - pair - 1))
 
     loads = [
         pltpu.make_async_copy(src, dst, load_sem.at[n])
@@ -48,8 +69,8 @@
             ((k_hbm, k_ref), (v_hbm, v_ref), (q_hbm, q_ref), (g_hbm, g_ref))
         )
     ]
-    for load in loads:
-        load.start()
+    loads[0].start()
+    loads[1].start()
 
     barrier = pltpu.get_barrier_semaphore()
     pl.semaphore_signal(barrier, inc=1, device_id={"seq": partner}, device_id_type=MESH)
@@ -62,7 +83,16 @@
     def _():
         pl.semaphore_signal(barrier, inc=1, device_id={"seq": me + 2}, device_id_type=MESH)
 
-    pl.semaphore_wait(barrier, 1 + has_far.astype(jnp.int32) + has_next.astype(jnp.int32))
+    @pl.when(pair >= 1)
+    def _():
+        pl.semaphore_signal(barrier, inc=1, device_id={"seq": me - 4}, device_id_type=MESH)
+
+    @pl.when(pair + 1 < pairs)
+    def _():
+        pl.semaphore_signal(barrier, inc=1, device_id={"seq": me + 4}, device_id_type=MESH)
+
+    greeted = [has_far, has_next, pair >= 1, pair + 1 < pairs]
+    pl.semaphore_wait(barrier, 1 + sum(g.astype(jnp.int32) for g in greeted))
 
     def remote(src, dst, send, recv, h, to):
         return pltpu.make_async_remote_copy(
@@ -73,6 +103,39 @@
     def far_copy(h):
         return remote(own, far, far_send, far_recv, h, me + 2)
 
+    def far_detour(h):
+        return remote(own, relay, far_send, relay_recv, h, me + 4)
+
+    def far_relay(h):
+        return remote(relay, far, relay_send, far_recv, h, me - 2)
+
+    def gfar_detour(h):
+        return remote(gfar_out, relay, gfar_send, relay_recv, h, me - 4)
+
+    def gfar_relay(h):
+        return remote(relay, gfar_in, relay_send, gfar_recv, h, me + 2)
+
+    def relay_forward(h):
+        @pl.when(relays_forward(h))
+        def _():
+            far_detour(h).wait_recv()
+            far_relay(h).start()
+
+    def relay_back(h):
+        @pl.when(relays_back(h))
+        def _():
+            gfar_detour(h).wait_recv()
+            gfar_relay(h).start()
+
+    def send_back(h):
+        @pl.when(detours_back(h))
+        def _():
+            gfar_detour(h).start()
+
+        @pl.when(jnp.logical_not(detours_back(h)))
+        def _():
+            gfar_copy(h).start()
+
     def near_own(h):
         return remote(own, near, near_send, near_recv, h, partner)
 
@@ -87,12 +150,18 @@
 
     loads[0].wait()
     loads[1].wait()
+    loads[2].start()
+    loads[3].start()
 
     def send_own(h, _):
         own[h, 0:tokens] = k_ref[pl.ds(h, tokens, stride=kheads), :].astype(BF16)
         own[h, tokens:] = v_ref[pl.ds(h, tokens, stride=kheads), :].astype(BF16)
 
-        @pl.when(has_next)
+        @pl.when(detours_forward(h))
+        def _():
+            far_detour(h).start()
+
+        @pl.when(jnp.logical_and(has_next, jnp.logical_not(detours_forward(h))))
         def _():
             far_copy(h).start()
 
@@ -102,7 +171,8 @@
 
         return 0
 
-    lax.fori_loop(0, kheads, send_own, 0)
+    early = min(3, kheads)
+    lax.fori_loop(0, early, send_own, 0)
     loads[2].wait()
     loads[3].wait()
 
@@ -145,9 +215,14 @@
         slot = lax.rem(h, 2)
         gnear_copy(h).wait_recv()
         gfar_out[h] = (held[slot] + gnear_in[h].astype(F32)).astype(BF16)
-        gfar_copy(h).start()
+        send_back(h)
 
     def step(h, _):
+        for later in (early, early + 1):
+            @pl.when(2 * h + later < kheads)
+            def _():
+                send_own(2 * h + later, 0)
+
         @pl.when(jnp.logical_and(core == 1, has_far))
         def _():
             far_copy(h).wait_recv()
@@ -166,6 +241,14 @@
 
         block("own", h, own, emit_own)
 
+        @pl.when(h == 0)
+        def _():
+            relay_forward(0)
+
+        @pl.when(h + 1 < kheads)
+        def _():
+            relay_forward(h + 1)
+
         @pl.when(has_near)
         def _():
             jax.lax.cond(
@@ -202,11 +285,16 @@
             @pl.when(core == 0)
             def _():
                 gfar_out[h] = held[slot].astype(BF16)
-                gfar_copy(h).start()
+                send_back(h)
 
         for g in range(group):
             at = pl.ds(h * group + g, tokens, stride=qheads)
             dq_ref[at, :] = dq_acc[g * tokens:(g + 1) * tokens] * SCALE
+
+        @pl.when(h >= 2)
+        def _():
+            relay_back(h - 2)
+
         return 0
 
     lax.fori_loop(0, kheads, step, 0)
@@ -217,6 +305,8 @@
 
     store = pltpu.make_async_copy(dq_ref, dq_hbm, store_sem)
     store.start()
+    for h in range(max(kheads - 2, 0), kheads):
+        relay_back(h)
 
     def finish(h, _):
         at = pl.ds(h, tokens, stride=kheads)
@@ -253,6 +343,10 @@
         @pl.when(has_far)
         def _():
             gfar_copy(h).wait_send()
+
+        @pl.when(jnp.logical_or(relays_forward(h), relays_back(h)))
+        def _():
+            far_relay(h).wait_send()
 
         return 0
 
@@ -264,7 +358,7 @@
     tokens, qheads, width = query.shape
     kheads = key.shape[1]
     group = qheads // kheads
-    assert WINDOW == 2 * tokens
+    assert WINDOW == 2 * tokens and devices % 4 == 0
     flat_q = (tokens * qheads, width)
     flat_k = (tokens * kheads, width)
     message = pltpu.VMEM((kheads, 2 * tokens, width), BF16)
@@ -286,14 +380,14 @@
             pltpu.VMEM(flat_k, F32),
             pltpu.VMEM(flat_q, F32),
             pltpu.VMEM(flat_q, F32),
-        ] + [message] * 7 + [
+        ] + [message] * 8 + [
             pltpu.VMEM((2, 2 * tokens, width), F32),
             pltpu.VMEM((group * tokens, width), F32),
             pltpu.VMEM((group * tokens, width), BF16),
             pltpu.VMEM((group * tokens, width), BF16),
             pltpu.SemaphoreType.DMA((4,)),
             pltpu.SemaphoreType.DMA,
-        ] + [sems] * 8,
+        ] + [sems] * 10,
         compiler_params=pltpu.CompilerParams(
             collective_id=0, has_side_effects=True, vmem_limit_bytes=58 * 2**20
         ),

time: 121 us -> 119 us (0.983); the launches traced: 120 us -> 119 us
  no operation moved by 1% of the time
where the time goes in v2:
time: 119 us
  Pallas kernels  110 us (92%)
  local copies, waits for them, and re-layouts  8.29 us (7%)
    pallas_call x1, Pallas kernels, on_device(): pl.pallas_call(functools.partial(kernel, tokens, kheads, group, devices),...  110 us
    unnamed x7, local copies, waits for them, and re-layouts  8.29 us

profile of v2, /device:TPU:0, one launch (start us, length us, event | category | flops | bytes accessed | tf_op | source)
XLA Modules:
  0.0 119.2 jit_solution(12308702879056700697)
XLA Ops:
  0.6 110.3 %shard_map.85 = (f32[8192,128]{1,0:T(8,128)}, f32[4096,128]{1,0:T(8,128)}, f32[4096,128]{1,0:T(8,128)}) custom-call(f32[8192,128]{1,0:T(8,128)} %bitcast.10, f32[4096,128]{1,0:T(8,128)} %bitcast.12, f32[4096,128]{1,0:T(8,128)} %bitcast.13, f32[8192,128]{1,0:T(8,128)} %bitcast.11, f32[16,512]{1,0:T(8,128)} %lse_ref.1, f32[16,512]{1,0:T(8,128)} %dots_ref.1), custom_call_target="tpu_custom_call" | custom-call | flops 10737418240 | bytes 20971520 | tf_op jit(solution)/shard_map/pallas_call | solution.py:368
  110.9 0.0 copy-start.1
  110.9 4.6 %copy.12 = f32[512,16,128]{2,1,0:T(8,128)} copy(f32[512,16,128]{2,1,0:T(8,128)} %bitcast.7) | data formatting | bytes 8388608
  115.5 0.0 copy-done.1
  115.5 0.0 copy-start
  115.5 1.3 %copy.13 = f32[512,8,128]{2,1,0:T(8,128)} copy(f32[512,8,128]{2,1,0:T(8,128)S(1)} %bitcast.9) | data formatting | bytes 4194304
  116.9 1.0 copy-done
  117.9 1.3 %copy.14 = f32[512,8,128]{2,1,0:T(8,128)} copy(f32[512,8,128]{2,1,0:T(8,128)S(1)} %bitcast.8) | data formatting | bytes 4194304
Async XLA Ops:
  110.9 4.6 %copy-start.1 = (f32[4096,128]{1,0:T(8,128)S(1)}, f32[4096,128]{1,0:T(8,128)}, u32[]{:S(2)}) copy-start(f32[4096,128]{1,0:T(8,128)} %get-tuple-element.7) | copy-start | bytes 6291460
  115.5 2.3 %copy-start = (f32[4096,128]{1,0:T(8,128)S(1)}, f32[4096,128]{1,0:T(8,128)}, u32[]{:S(2)}) copy-start(f32[4096,128]{1,0:T(8,128)} %get-tuple-element.8) | copy-start | bytes 6291460

commit v3 on v2

--- a/solution.py
+++ b/solution.py
@@ -27,7 +27,7 @@
     dq_hbm, dk_ref, dv_ref,
     q_ref, k_ref, v_ref, g_ref, dq_ref,
     own, far, near, relay, gnear_out, gnear_in, gfar_out, gfar_in,
-    held, dq_acc, qb, gb,
+    held, dq_acc, qb, gb, qt, gt,
     load_sem, store_sem,
     far_send, far_recv, near_send, near_recv,
     gnear_send, gnear_recv, gfar_send, gfar_recv, relay_send, relay_recv,
@@ -177,39 +177,62 @@
     loads[3].wait()
 
     def block(kind, h, kv, emit):
-        for jb in range(2):
+        halves = {"own": ((0, 1), (1,)), "near": ((0, 1), (0, 1)), "far": ((0,), (0, 1))}[kind]
+        kt = kv[h, 0:tokens].T
+        ps, dss = {}, {}
+
+        def scores(jb, g):
+            lo, hi = halves[jb][0] * half, (halves[jb][-1] + 1) * half
+            cols = slice(g * tokens + lo, g * tokens + hi)
             k = kv[h, jb * half:(jb + 1) * half]
             v = kv[h, tokens + jb * half:tokens + (jb + 1) * half]
-            dk = dv = None
-            for g in range(group):
-                lo, hi = 0, tokens
+            lse = lse_ref[pl.ds(h * group + g, 1), lo:hi]
+            dots = dots_ref[pl.ds(h * group + g, 1), lo:hi]
+            s = dot(k, qt[:, cols], 1, 0)
+            p = jnp.exp2(s * (SCALE * LOG2E) - lse * LOG2E)
+            if kind != "near":
+                kpos = lax.broadcasted_iota(jnp.int32, p.shape, 0) + jb * half
+                qpos = lax.broadcasted_iota(jnp.int32, p.shape, 1) + lo
+                keep = qpos >= kpos if kind == "own" else qpos < kpos
+                p = jnp.where(keep, p, 0.0)
+            ds = p * (dot(v, gt[:, cols], 1, 0) - dots)
+            ps[jb, g] = p.astype(BF16)
+            dss[jb, g] = ds.astype(BF16)
+
+        def key_terms(jb):
+            lo, hi = halves[jb][0] * half, (halves[jb][-1] + 1) * half
+            rows = [slice(g * tokens + lo, g * tokens + hi) for g in range(group)]
+            p = jnp.concatenate([ps[jb, g] for g in range(group)], axis=1)
+            ds = jnp.concatenate([dss[jb, g] for g in range(group)], axis=1)
+            go = jnp.concatenate([gb[r] for r in rows], axis=0)
+            q = jnp.concatenate([qb[r] for r in rows], axis=0)
+            emit(jb, dot(ds, q, 1, 0) * SCALE, dot(p, go, 1, 0))
+
+        def query_terms(g):
+            for ib in range(2):
+                jbs = [jb for jb in range(2) if ib in halves[jb]]
+                parts = []
+                for jb in jbs:
+                    at = (ib - halves[jb][0]) * half
+                    parts.append(dss[jb, g][:, at:at + half])
+                ds = parts[0] if len(parts) == 1 else jnp.concatenate(parts, axis=0)
+                dq = dot(kt[:, jbs[0] * half:(jbs[-1] + 1) * half], ds, 1, 0)
+                cols = slice(g * tokens + ib * half, g * tokens + (ib + 1) * half)
                 if kind == "own":
-                    lo = jb * half
-                elif kind == "far":
-                    hi = (jb + 1) * half
-                rows = slice(g * tokens + lo, g * tokens + hi)
-                q = qb[rows]
-                go = gb[rows]
-                lse = lse_ref[pl.ds(h * group + g, 1), lo:hi]
-                dots = dots_ref[pl.ds(h * group + g, 1), lo:hi]
-                s = dot(k, q, 1, 1)
-                p = jnp.exp2(s * (SCALE * LOG2E) - lse * LOG2E)
-                if kind != "near":
-                    kpos = lax.broadcasted_iota(jnp.int32, p.shape, 0) + jb * half
-                    qpos = lax.broadcasted_iota(jnp.int32, p.shape, 1) + lo
-                    keep = qpos >= kpos if kind == "own" else qpos < kpos
-                    p = jnp.where(keep, p, 0.0)
-                ds = (p * (dot(v, go, 1, 1) - dots)).astype(BF16)
-                dv_term = dot(p.astype(BF16), go, 1, 0)
-                dk_term = dot(ds, q, 1, 0)
-                dv = dv_term if dv is None else dv + dv_term
-                dk = dk_term if dk is None else dk + dk_term
-                dq = dot(ds, k, 0, 0)
-                if kind == "own" and jb == 0:
-                    dq_acc[rows] = dq
+                    dq_acc[:, cols] = dq
                 else:
-                    dq_acc[rows] += dq
-            emit(jb, dk * SCALE, dv)
+                    dq_acc[:, cols] += dq
+
+        for g in range(group):
+            scores(0, g)
+        scores(1, 0)
+        key_terms(0)
+        for g in range(1, group):
+            scores(1, g)
+        query_terms(0)
+        key_terms(1)
+        for g in range(1, group):
+            query_terms(g)
 
     def send_sum(h):
         slot = lax.rem(h, 2)
@@ -231,8 +254,12 @@
         for g in range(group):
             rows = slice(g * tokens, (g + 1) * tokens)
             at = pl.ds(h * group + g, tokens, stride=qheads)
-            qb[rows] = q_ref[at, :].astype(BF16)
-            gb[rows] = g_ref[at, :].astype(BF16)
+            q = q_ref[at, :]
+            go = g_ref[at, :]
+            qb[rows] = q.astype(BF16)
+            gb[rows] = go.astype(BF16)
+            qt[:, rows] = q.T.astype(BF16)
+            gt[:, rows] = go.T.astype(BF16)
 
         def emit_own(jb, dk, dv):
             at = pl.ds(jb * half * kheads + h, half, stride=kheads)
@@ -289,7 +316,7 @@
 
         for g in range(group):
             at = pl.ds(h * group + g, tokens, stride=qheads)
-            dq_ref[at, :] = dq_acc[g * tokens:(g + 1) * tokens] * SCALE
+            dq_ref[at, :] = dq_acc[:, g * tokens:(g + 1) * tokens].T * SCALE
 
         @pl.when(h >= 2)
         def _():
@@ -382,9 +409,11 @@
             pltpu.VMEM(flat_q, F32),
         ] + [message] * 8 + [
             pltpu.VMEM((2, 2 * tokens, width), F32),
-            pltpu.VMEM((group * tokens, width), F32),
+            pltpu.VMEM((width, group * tokens), F32),
             pltpu.VMEM((group * tokens, width), BF16),
             pltpu.VMEM((group * tokens, width), BF16),
+            pltpu.VMEM((width, group * tokens), BF16),
+            pltpu.VMEM((width, group * tokens), BF16),
             pltpu.SemaphoreType.DMA((4,)),
             pltpu.SemaphoreType.DMA,
         ] + [sems] * 10,

time: 119 us -> 118 us (level)
  no operation moved by 1% of the time
where the time goes in v3:
time: 118 us
  Pallas kernels  109 us (92%)
  local copies, waits for them, and re-layouts  8.29 us (7%)
    pallas_call x1, Pallas kernels, on_device(): pl.pallas_call(functools.partial(kernel, tokens, kheads, group, devices),...  109 us
    unnamed x7, local copies, waits for them, and re-layouts  8.29 us

profile of v3, /device:TPU:0, one launch (start us, length us, event | category | flops | bytes accessed | tf_op | source)
XLA Modules:
  0.0 118.3 jit_solution(8372714912013137454)
XLA Ops:
  0.6 109.3 %shard_map.85 = (f32[8192,128]{1,0:T(8,128)}, f32[4096,128]{1,0:T(8,128)}, f32[4096,128]{1,0:T(8,128)}) custom-call(f32[8192,128]{1,0:T(8,128)} %bitcast.10, f32[4096,128]{1,0:T(8,128)} %bitcast.12, f32[4096,128]{1,0:T(8,128)} %bitcast.13, f32[8192,128]{1,0:T(8,128)} %bitcast.11, f32[16,512]{1,0:T(8,128)} %lse_ref.1, f32[16,512]{1,0:T(8,128)} %dots_ref.1), custom_call_target="tpu_custom_call" | custom-call | flops 10737418240 | bytes 20971520 | tf_op jit(solution)/shard_map/pallas_call | solution.py:395
  110.0 0.0 copy-start.1
  110.0 4.6 %copy.12 = f32[512,16,128]{2,1,0:T(8,128)} copy(f32[512,16,128]{2,1,0:T(8,128)} %bitcast.7) | data formatting | bytes 8388608
  114.6 0.0 copy-done.1
  114.6 0.0 copy-start
  114.6 1.3 %copy.13 = f32[512,8,128]{2,1,0:T(8,128)} copy(f32[512,8,128]{2,1,0:T(8,128)S(1)} %bitcast.9) | data formatting | bytes 4194304
  115.9 1.0 copy-done
  117.0 1.3 %copy.14 = f32[512,8,128]{2,1,0:T(8,128)} copy(f32[512,8,128]{2,1,0:T(8,128)S(1)} %bitcast.8) | data formatting | bytes 4194304
Async XLA Ops:
  110.0 4.6 %copy-start.1 = (f32[4096,128]{1,0:T(8,128)S(1)}, f32[4096,128]{1,0:T(8,128)}, u32[]{:S(2)}) copy-start(f32[4096,128]{1,0:T(8,128)} %get-tuple-element.7) | copy-start | bytes 6291460
  114.6 2.3 %copy-start = (f32[4096,128]{1,0:T(8,128)S(1)}, f32[4096,128]{1,0:T(8,128)}, u32[]{:S(2)}) copy-start(f32[4096,128]{1,0:T(8,128)} %get-tuple-element.8) | copy-start | bytes 6291460

commit v4 on v3

--- a/solution.py
+++ b/solution.py
@@ -24,8 +24,8 @@
 def kernel(
     tokens, kheads, group, devices,
     q_hbm, k_hbm, v_hbm, g_hbm, lse_ref, dots_ref,
-    dq_hbm, dk_ref, dv_ref,
-    q_ref, k_ref, v_ref, g_ref, dq_ref,
+    dq_hbm, dk_out, dv_out,
+    q_ref, k_ref, v_ref, g_ref, dq_ref, dk_ref, dv_ref, dq_low,
     own, far, near, relay, gnear_out, gnear_in, gfar_out, gfar_in,
     held, dq_acc, qb, gb, qt, gt,
     load_sem, store_sem,
@@ -171,8 +171,7 @@
 
         return 0
 
-    early = min(3, kheads)
-    lax.fori_loop(0, early, send_own, 0)
+    lax.fori_loop(0, kheads, send_own, 0)
     loads[2].wait()
     loads[3].wait()
 
@@ -241,11 +240,6 @@
         send_back(h)
 
     def step(h, _):
-        for later in (early, early + 1):
-            @pl.when(2 * h + later < kheads)
-            def _():
-                send_own(2 * h + later, 0)
-
         @pl.when(jnp.logical_and(core == 1, has_far))
         def _():
             far_copy(h).wait_recv()
@@ -330,10 +324,17 @@
     def _():
         send_sum(kheads - 1)
 
-    store = pltpu.make_async_copy(dq_ref, dq_hbm, store_sem)
-    store.start()
     for h in range(max(kheads - 2, 0), kheads):
         relay_back(h)
+
+    def round_query(n, _):
+        rows = pl.ds(pl.multiple_of(n * tokens, tokens), tokens)
+        dq_low[rows] = dq_ref[rows].astype(BF16)
+        return 0
+
+    lax.fori_loop(0, qheads, round_query, 0)
+    store = pltpu.make_async_copy(dq_low, dq_hbm, store_sem)
+    store.start()
 
     def finish(h, _):
         at = pl.ds(h, tokens, stride=kheads)
@@ -353,6 +354,14 @@
         return 0
 
     lax.fori_loop(0, kheads, finish, 0)
+
+    def round_keys(n, _):
+        rows = pl.ds(pl.multiple_of(n * tokens, tokens), tokens)
+        dk_out[rows] = dk_ref[rows].astype(BF16)
+        dv_out[rows] = dv_ref[rows].astype(BF16)
+        return 0
+
+    lax.fori_loop(0, kheads, round_keys, 0)
 
     def drain(h, _):
         @pl.when(has_next)
@@ -395,9 +404,9 @@
     dq, dk, dv = pl.pallas_call(
         functools.partial(kernel, tokens, kheads, group, devices),
         out_shape=(
-            jax.ShapeDtypeStruct(flat_q, F32),
-            jax.ShapeDtypeStruct(flat_k, F32),
-            jax.ShapeDtypeStruct(flat_k, F32),
+            jax.ShapeDtypeStruct(flat_q, BF16),
+            jax.ShapeDtypeStruct(flat_k, BF16),
+            jax.ShapeDtypeStruct(flat_k, BF16),
         ),
         in_specs=[anywhere] * 4 + [vmem] * 2,
         out_specs=(anywhere, vmem, vmem),
@@ -407,6 +416,9 @@
             pltpu.VMEM(flat_k, F32),
             pltpu.VMEM(flat_q, F32),
             pltpu.VMEM(flat_q, F32),
+            pltpu.VMEM(flat_k, F32),
+            pltpu.VMEM(flat_k, F32),
+            pltpu.VMEM(flat_q, BF16),
         ] + [message] * 8 + [
             pltpu.VMEM((2, 2 * tokens, width), F32),
             pltpu.VMEM((width, group * tokens), F32),
@@ -429,7 +441,11 @@
         query.reshape(flat_q), key.reshape(flat_k), value.reshape(flat_k),
         gradient.reshape(flat_q), logsumexp, dots,
     )
-    return dq.reshape(query.shape), dk.reshape(key.shape), dv.reshape(value.shape)
+    return (
+        dq.astype(F32).reshape(query.shape),
+        dk.astype(F32).reshape(key.shape),
+        dv.astype(F32).reshape(value.shape),
+    )
 
 
 def solution(mesh):

time: 118 us -> 116 us (0.983)
  local copies, waits for them, and re-layouts: 8.29 us -> 0.01 us
  other arithmetic: 0 us -> 6.31 us
    unnamed x7 -> x2, local copies, waits for them, and re-layouts: 8.29 us -> 0.01 us
    reshape x0 -> x2, other arithmetic: none -> 6.31 us  [the longest x1 3.97 us: on_device(): dv.astype(F32).reshape(value.shape)]
where the time goes in v4:
time: 116 us
  Pallas kernels  109 us (94%)
  other arithmetic  6.31 us (5%)
    pallas_call x1, Pallas kernels, on_device(): pl.pallas_call(functools.partial(kernel, tokens, kheads, group, devices),...  109 us
    reshape x1, other arithmetic, on_device(): dv.astype(F32).reshape(value.shape)  3.97 us
    reshape x1, other arithmetic, on_device(): dq.astype(F32).reshape(query.shape)  2.34 us

profile of v4, /device:TPU:0, one launch (start us, length us, event | category | flops | bytes accessed | tf_op | source)
XLA Modules:
  0.0 115.6 jit_solution(387087755623950654)
XLA Ops:
  0.6 108.6 %shard_map.85 = (bf16[8192,128]{1,0:T(8,128)(2,1)}, bf16[4096,128]{1,0:T(8,128)(2,1)}, bf16[4096,128]{1,0:T(8,128)(2,1)}) custom-call(f32[8192,128]{1,0:T(8,128)} %bitcast.13, f32[4096,128]{1,0:T(8,128)} %bitcast.15, f32[4096,128]{1,0:T(8,128)} %bitcast.16, f32[8192,128]{1,0:T(8,128)} %bitcast.14, f32[16,512]{1,0:T(8,128)} %lse_ref.1, f32[16,512]{1,0:T(8,128)} %dots_ref.1), custom_call_target="tpu_custom_call" | custom-call | flops 10737418240 | bytes 20971520 | tf_op jit(solution)/shard_map/pallas_call | solution.py:404
  109.2 0.0 copy-start
  109.3 4.0 %bitcast_convert_fusion = (f32[512,8,128]{2,1,0:T(8,128)}, f32[512,8,128]{2,1,0:T(8,128)}) fusion(bf16[4096,128]{1,0:T(8,128)(2,1)} %get-tuple-element.8, bf16[4096,128]{1,0:T(8,128)(2,1)} %get-tuple-element.7), kind=kLoop, calls=%fused_computation | loop fusion | flops 1048576 | bytes 6291456 | tf_op jit(solution)/shard_map/reshape | solution.py:447
  113.2 0.0 copy-done
  113.2 2.3 %convert.3 = f32[512,16,128]{2,1,0:T(8,128)} convert(bf16[512,16,128]{2,1,0:T(8,128)(2,1)S(1)} %bitcast.12) | non-fusion elementwise | flops 1048576 | bytes 6291456 | tf_op jit(solution)/shard_map/reshape | solution.py:445
Async XLA Ops:
  109.2 4.0 %copy-start = (bf16[8192,128]{1,0:T(8,128)(2,1)S(1)}, bf16[8192,128]{1,0:T(8,128)(2,1)}, u32[]{:S(2)}) copy-start(bf16[8192,128]{1,0:T(8,128)(2,1)} %get-tuple-element.6) | copy-start | bytes 6291460

commit v5 on v4

--- a/solution.py
+++ b/solution.py
@@ -58,10 +58,10 @@
         return both(odd, pair >= 1, picked(h + 3, pair))
 
     def detours_back(h):
-        return both(jnp.logical_not(odd), pair >= 1, picked(h, pairs - pair))
+        return both(jnp.logical_not(odd), pair >= 1, picked(h, jnp.minimum(pairs - pair, pairs // 2)))
 
     def relays_back(h):
-        return both(jnp.logical_not(odd), pair + 1 < pairs, picked(h, pairs - pair - 1))
+        return both(jnp.logical_not(odd), pair + 1 < pairs, picked(h, jnp.minimum(pairs - pair - 1, pairs // 2)))
 
     loads = [
         pltpu.make_async_copy(src, dst, load_sem.at[n])

time: 116 us -> 115 us (level)
  Pallas kernels: 109 us -> 107 us
    pallas_call x1, Pallas kernels: 109 us -> 107 us  [on_device(): pl.pallas_call(functools.partial(kernel, tokens, kheads, group, devices),...]
where the time goes in v5:
time: 115 us; the launch traced here: 114 us
  Pallas kernels  107 us (93%)
  other arithmetic  6.31 us (5%)
    pallas_call x1, Pallas kernels, on_device(): pl.pallas_call(functools.partial(kernel, tokens, kheads, group, devices),...  107 us
    reshape x1, other arithmetic, on_device(): dv.astype(F32).reshape(value.shape)  3.97 us
    reshape x1, other arithmetic, on_device(): dq.astype(F32).reshape(query.shape)  2.34 us

profile of v5, /device:TPU:0, one launch (start us, length us, event | category | flops | bytes accessed | tf_op | source)
XLA Modules:
  0.0 114.3 jit_solution(17478475747787951701)
XLA Ops:
  0.6 107.4 %shard_map.85 = (bf16[8192,128]{1,0:T(8,128)(2,1)}, bf16[4096,128]{1,0:T(8,128)(2,1)}, bf16[4096,128]{1,0:T(8,128)(2,1)}) custom-call(f32[8192,128]{1,0:T(8,128)} %bitcast.13, f32[4096,128]{1,0:T(8,128)} %bitcast.15, f32[4096,128]{1,0:T(8,128)} %bitcast.16, f32[8192,128]{1,0:T(8,128)} %bitcast.14, f32[16,512]{1,0:T(8,128)} %lse_ref.1, f32[16,512]{1,0:T(8,128)} %dots_ref.1), custom_call_target="tpu_custom_call" | custom-call | flops 10737418240 | bytes 20971520 | tf_op jit(solution)/shard_map/pallas_call | solution.py:404
  108.0 0.0 copy-start
  108.0 4.0 %bitcast_convert_fusion = (f32[512,8,128]{2,1,0:T(8,128)}, f32[512,8,128]{2,1,0:T(8,128)}) fusion(bf16[4096,128]{1,0:T(8,128)(2,1)} %get-tuple-element.8, bf16[4096,128]{1,0:T(8,128)(2,1)} %get-tuple-element.7), kind=kLoop, calls=%fused_computation | loop fusion | flops 1048576 | bytes 6291456 | tf_op jit(solution)/shard_map/reshape | solution.py:447
  112.0 0.0 copy-done
  112.0 2.3 %convert.3 = f32[512,16,128]{2,1,0:T(8,128)} convert(bf16[512,16,128]{2,1,0:T(8,128)(2,1)S(1)} %bitcast.12) | non-fusion elementwise | flops 1048576 | bytes 6291456 | tf_op jit(solution)/shard_map/reshape | solution.py:445
Async XLA Ops:
  108.0 4.0 %copy-start = (bf16[8192,128]{1,0:T(8,128)(2,1)S(1)}, bf16[8192,128]{1,0:T(8,128)(2,1)}, u32[]{:S(2)}) copy-start(bf16[8192,128]{1,0:T(8,128)(2,1)} %get-tuple-element.6) | copy-start | bytes 6291460
